TPU v7x, 32 devices: a whole 2x2x4 slice. The times are simulated.
32 devices in a mesh: src: 32 (over z, y, x, core), dst: 1.
Axes of the slice: x: 2, y: 2, z: 4, core: 2. Of those that a mesh axis runs over, the one named last changes fastest.
Arguments:
- out_density: float32 [16384], P('src'), may hold values from 0.008 to 0.08
- in_density: float32 [16384], P('dst'), may hold values from 0.008 to 0.08
- retention: float32 [16384], P('src'), may hold values from 0.15 to 0.75
- demand: float32 [16384], P('src'), may hold values from 0.5 to 4
- location: int32 [16384], replicated, may hold values from 0 to 16383
- scenario_blocks: int32 [32], replicated, may hold values from 0 to 127
Outputs:
- out_fitness: float32 [16384], P('src')
- in_fitness: float32 [16384], P('dst')
- levels: float32 [16384, 32], P('src', 'dst')
Inputs may be any that keep to these rules, and one draw needn't show every extreme that they name: `scenario_blocks`: scenario k extracts the 128 firms of block index b = scenario_blocks_k, firms 128 * b to 128 * b + 127. `location`: several firms may share a map cell, and some cells hold none.
All inputs are finite; a program needn't handle non-finite values.
Results may differ from a plain program's by a relative error of at most 0.0003.
Values sent between devices are 32-bit elements; how exact they have to be, the bound alone decides.
A program may use at most 64 MiB of HBM per device.

v0:
```python
import math
import jax
import jax.numpy as jnp
from jax import lax
from jax.sharding import PartitionSpec as P

SWEEPS = 2
ITERS = 2
EXTRACT = 128
MAP_SIDE = 256
RANGE = 18
far_weight = 0.015625


def on_device(out_density, in_density, retention, demand, location, scenario_blocks):
    rows_dev = out_density.shape[0]
    cols_dev = in_density.shape[0]
    firms = rows_dev * lax.axis_size("src")
    row_start = lax.axis_index("src") * rows_dev
    col_start = lax.axis_index("dst") * cols_dev
    height = math.gcd(rows_dev, 128)
    blocks = rows_dev // height
    col_ids = col_start + jnp.arange(cols_dev, dtype=jnp.int32)
    offsets = jnp.arange(blocks, dtype=jnp.int32) * height
    src_cells = lax.dynamic_slice_in_dim(location, row_start, rows_dev)
    dst_cells = lax.dynamic_slice_in_dim(location, col_start, cols_dev)
    src_row = src_cells // MAP_SIDE
    src_col = src_cells % MAP_SIDE
    dst_row = dst_cells // MAP_SIDE
    dst_col = dst_cells % MAP_SIDE
    out_fit = jnp.sqrt(out_density)
    in_fit = jnp.sqrt(in_density)

    def pair_weight(offset):
        row_ids = row_start + offset + jnp.arange(height, dtype=jnp.int32)
        row_gap = lax.dynamic_slice_in_dim(src_row, offset, height)[:, None] - dst_row[None, :]
        col_gap = lax.dynamic_slice_in_dim(src_col, offset, height)[:, None] - dst_col[None, :]
        nearby = row_gap * row_gap + col_gap * col_gap <= RANGE * RANGE
        affinity = jnp.where(nearby, 1.0, far_weight)
        return jnp.where(row_ids[:, None] != col_ids[None, :], affinity, 0.0)

    for sweep_no in range(SWEEPS):

        def row_part(offset):
            row_fit = lax.dynamic_slice_in_dim(out_fit, offset, height)
            weight = pair_weight(offset)
            ratios = weight * in_fit[None, :] / (1.0 + row_fit[:, None] * in_fit[None, :] * weight)
            return jnp.sum(ratios, axis=1)

        row_partial = lax.map(row_part, offsets).reshape(rows_dev)
        row_total = lax.psum(row_partial, "dst")
        out_fit = firms * out_density / row_total

        def col_part(running, offset):
            row_fit = lax.dynamic_slice_in_dim(out_fit, offset, height)
            weight = pair_weight(offset)
            ratios = weight * row_fit[:, None] / (1.0 + row_fit[:, None] * in_fit[None, :] * weight)
            return (running + jnp.sum(ratios, axis=0), None)

        col_partial, _ = lax.scan(col_part, jnp.zeros((cols_dev,), jnp.float32), offsets)
        col_total = lax.psum(col_partial, "src")
        in_fit = firms * in_density / col_total
    row_scale = retention / (firms * out_density)

    def coeff_block(offset):
        row_fit = lax.dynamic_slice_in_dim(out_fit, offset, height)
        scale_part = lax.dynamic_slice_in_dim(row_scale, offset, height)
        product = row_fit[:, None] * in_fit[None, :] * pair_weight(offset)
        chance = product / (1.0 + product)
        return chance * scale_part[:, None]

    coefficients = lax.map(coeff_block, offsets).reshape(rows_dev, cols_dev)
    scenarios = scenario_blocks.shape[0]
    portion = scenarios // lax.axis_size("dst")
    leading = lax.axis_index("dst") * portion
    firm_rows = row_start + jnp.arange(rows_dev, dtype=jnp.int32)
    retained = (firm_rows[:, None] // EXTRACT != scenario_blocks[None, :]).astype(jnp.float32)
    levels = retained * demand[:, None]
    for round_no in range(ITERS):
        every_row = lax.all_gather(levels, "src", axis=0, tiled=True)
        columns = lax.dynamic_slice_in_dim(every_row, col_start, cols_dev, 0)
        summed = lax.psum(
            jnp.dot(
                coefficients,
                columns,
                preferred_element_type=jnp.float32,
                precision=lax.Precision.HIGHEST,
            ),
            "dst",
        )
        levels = retained * (demand[:, None] + summed)
    result = lax.dynamic_slice_in_dim(levels, leading, portion, 1)
    return (out_fit, in_fit, result)


def solution(mesh):
    in_specs = (P("src"), P("dst"), P("src"), P("src"), P(), P())
    out_specs = (P("src"), P("dst"), P("src", "dst"))
    return jax.shard_map(
        on_device, mesh=mesh, in_specs=in_specs, out_specs=out_specs, check_vma=False
    )
```

profile of v0, /device:TPU:0, one launch (start us, length us, event | category | flops | bytes accessed | tf_op | source)
XLA Modules:
  0.0 580.2 jit_solution(1393125838560426272)
XLA Ops:
  10.5 33.4 %while.55 = (s32[]{:T(128)}, f32[4,128]{1,0:T(4,128)S(1)}, s32[4]{0:T(128)S(1)}, s32[]{:T(128)}, s32[512]{0:T(512)S(1)}, /*index=5*/s32[16384]{0:T(1024)S(1)}, s...) while((s32[]{:T(128)}, f32[4,128]{1,0:T(4,128)S(1)}, ...), condition=%wide.region_2.3_spmd.clone, body=%wide.region_0.2_spmd.clone.sunk | while | flops 31457284 | bytes 203979 | solution.py:50
  22.3 4.9 fusion.33
  44.6 34.3 %while.58 = (s32[]{:T(128)}, f32[16384]{0:T(1024)S(1)}, s32[4]{0:T(128)S(1)}, s32[]{:T(128)}, s32[512]{0:T(512)S(1)}, /*index=5*/s32[16384]{0:T(1024)S(1)}, s32[...) while((s32[]{:T(128)}, f32[16384]{0:T(1024)S(1)}, ...), condition=%wide.region_5.6_spmd.clone, body=%wide.region_3.5_spmd.clone.sunk | while | flops 31473796 | bytes 464593 | solution.py:60
  48.0 5.1 fusion.36
  56.6 5.1 fusion.36
  65.2 5.1 fusion.36
  73.8 5.1 fusion.36
  79.7 120.3 %all-reduce.3.cloned.1.call-done = f32[16384]{0:T(1024)} async-done(((f32[16384]{0:T(1024)}), f32[16384]{0:T(1024)}) %all-reduce.3.cloned.1.call-update) | async-done | bytes 65552 | tf_op jit(solution)/shard_map/psum | solution.py:61
  200.9 33.4 %while.56 = (s32[]{:T(128)}, f32[4,128]{1,0:T(4,128)S(1)}, s32[4]{0:T(128)S(1)}, s32[]{:T(128)}, s32[512]{0:T(512)S(1)}, /*index=5*/s32[16384]{0:T(1024)S(1)}, s...) while((s32[]{:T(128)}, f32[4,128]{1,0:T(4,128)S(1)}, ...), condition=%wide.region_9.10_spmd.clone, body=%wide.region_7.9_spmd.clone.sunk | while | flops 31457284 | bytes 203979 | solution.py:50
  235.0 34.3 %while.59 = (s32[]{:T(128)}, f32[16384]{0:T(1024)S(1)}, s32[4]{0:T(128)S(1)}, s32[]{:T(128)}, s32[512]{0:T(512)S(1)}, /*index=5*/s32[16384]{0:T(1024)S(1)}, s32[...) while((s32[]{:T(128)}, f32[16384]{0:T(1024)S(1)}, ...), condition=%wide.region_12.13_spmd.clone, body=%wide.region_10.12_spmd.clone.sunk | while | flops 31473796 | bytes 464593 | solution.py:60
  238.4 5.1 fusion.37
  247.0 5.1 fusion.37
  255.6 5.1 fusion.37
  264.2 5.1 fusion.37
  271.0 117.5 %all-reduce.5.cloned.1.call-done = f32[16384]{0:T(1024)} async-done(((f32[16384]{0:T(1024)}), f32[16384]{0:T(1024)}) %all-reduce.5.cloned.1.call-update) | async-done | bytes 65552 | tf_op jit(solution)/shard_map/psum | solution.py:61
  389.4 39.0 %while.57 = (s32[]{:T(128)}, f32[4,128,16384]{2,1,0:T(8,128)}, s32[4]{0:T(128)S(1)}, f32[512]{0:T(512)S(1)}, f32[16384]{0:T(1024)S(1)}, /*index=5*/s32[]{:T(128)...) while((s32[]{:T(128)}, f32[4,128,16384]{2,1,0:T(8,128)}, ...), condition=%wide.region_15.16_spmd.clone, body=%wide.region_14.15_spmd.clone.sunk | while | flops 29360260 | bytes 8593107 | solution.py:72
  392.9 6.3 %fusion.35 = f32[4,128,16384]{2,1,0:T(8,128)} fusion(f32[4,128,16384]{2,1,0:T(8,128)} %get-tuple-element.1026, s32[]{:T(128)} %get-tuple-element.1025, f32[128]{0:T(128)S(1)} %dynamic_slice.129, s32[16384]{0:T(1024)S(1)} %get-tuple-element.1048, s32[128]{0:T(128)S(1)} %dynamic_slice.130, s32[16384]{0:T(1024)S(1)} %get-tuple-element.1046, ...), kind=kLoop, calls=%fused_computation.17.clone.1 | loop fusion | flops 29360128 | bytes 8588288 | tf_op jit(solution)/shard_map/while/body/jit(dynamic_update_index_in_dim)/dynamic_update_slice | solution.py:72
  402.6 6.2 %fusion.35 = f32[4,128,16384]{2,1,0:T(8,128)} fusion(f32[4,128,16384]{2,1,0:T(8,128)} %get-tuple-element.1026, s32[]{:T(128)} %get-tuple-element.1025, f32[128]{0:T(128)S(1)} %dynamic_slice.129, s32[16384]{0:T(1024)S(1)} %get-tuple-element.1048, s32[128]{0:T(128)S(1)} %dynamic_slice.130, s32[16384]{0:T(1024)S(1)} %get-tuple-element.1046, ...), kind=kLoop, calls=%fused_computation.17.clone.1 | loop fusion | flops 29360128 | bytes 8588288 | tf_op jit(solution)/shard_map/while/body/jit(dynamic_update_index_in_dim)/dynamic_update_slice | solution.py:72
  412.4 6.3 %fusion.35 = f32[4,128,16384]{2,1,0:T(8,128)} fusion(f32[4,128,16384]{2,1,0:T(8,128)} %get-tuple-element.1026, s32[]{:T(128)} %get-tuple-element.1025, f32[128]{0:T(128)S(1)} %dynamic_slice.129, s32[16384]{0:T(1024)S(1)} %get-tuple-element.1048, s32[128]{0:T(128)S(1)} %dynamic_slice.130, s32[16384]{0:T(1024)S(1)} %get-tuple-element.1046, ...), kind=kLoop, calls=%fused_computation.17.clone.1 | loop fusion | flops 29360128 | bytes 8588288 | tf_op jit(solution)/shard_map/while/body/jit(dynamic_update_index_in_dim)/dynamic_update_slice | solution.py:72
  422.1 6.2 %fusion.35 = f32[4,128,16384]{2,1,0:T(8,128)} fusion(f32[4,128,16384]{2,1,0:T(8,128)} %get-tuple-element.1026, s32[]{:T(128)} %get-tuple-element.1025, f32[128]{0:T(128)S(1)} %dynamic_slice.129, s32[16384]{0:T(1024)S(1)} %get-tuple-element.1048, s32[128]{0:T(128)S(1)} %dynamic_slice.130, s32[16384]{0:T(1024)S(1)} %get-tuple-element.1046, ...), kind=kLoop, calls=%fused_computation.17.clone.1 | loop fusion | flops 29360128 | bytes 8588288 | tf_op jit(solution)/shard_map/while/body/jit(dynamic_update_index_in_dim)/dynamic_update_slice | solution.py:72
  428.3 20.0 %all-gather.3.cloned.1.call-done = f32[16384,32]{0,1:T(8,128)} async-done(((f32[512,32]{0,1:T(8,128)}), f32[16384,32]{0,1:T(8,128)}) %all-gather.3.cloned.1.call-update) | async-done | bytes 2097168 | tf_op jit(solution)/shard_map/all_gather | solution.py:80
  448.4 35.0 %fusion.17 = f32[512,32]{0,1:T(8,128)} fusion(f32[512,16384]{1,0:T(8,128)} %bitcast.30, f32[16384,32]{0,1:T(8,128)} %all-gather.3.cloned.1.call-done, f32[512]{0:T(512)S(1)} %copy-done.4, s32[512]{0:T(512)S(1)} %add_select_fusion.2, s32[32]{0:T(128)S(1)} %copy-done.5), kind=kOutput, calls=%fused_computation.36 | convolution fusion | flops 3221274624 | bytes 35721344 | tf_op jit(solution)/shard_map/dot_general | solution.py:83
  483.4 55.3 %all-gather.5.cloned.1.call-done = f32[16384,32]{0,1:T(8,128)} async-done(((f32[512,32]{0,1:T(8,128)}), f32[16384,32]{0,1:T(8,128)}) %all-gather.5.cloned.1.call-update) | async-done | bytes 2097168 | tf_op jit(solution)/shard_map/all_gather | solution.py:80
  538.7 35.0 %fusion.16 = f32[512,32]{0,1:T(8,128)} fusion(f32[512,16384]{1,0:T(8,128)} %bitcast.31, f32[16384,32]{0,1:T(8,128)} %all-gather.5.cloned.1.call-done, f32[512]{0:T(512)S(1)} %copy-done.4, s32[512]{0:T(512)S(1)} %add_select_fusion.2, s32[32]{0:T(128)S(1)} %copy-done.5), kind=kOutput, calls=%fused_computation.34 | convolution fusion | flops 3221274624 | bytes 35721344 | tf_op jit(solution)/shard_map/dot_general | solution.py:83
  (165 shorter events, 60.0 us)
Async XLA Ops:
  7.2 381.3 %copy-start.3 = (f32[16384]{0:T(1024)S(1)}, f32[16384]{0:T(1024)}, u32[]{:S(2)}) copy-start(f32[16384]{0:T(1024)} %param.17) | copy-start | bytes 196612
  7.2 262.9 %copy-start.4 = (f32[512]{0:T(512)S(1)}, f32[512]{0:T(512)}, u32[]{:S(2)}) copy-start(f32[512]{0:T(512)} %param.19) | copy-start | bytes 6148
  7.2 262.9 %copy-start.5 = (s32[32]{0:T(128)S(1)}, s32[32]{0:T(128)}, u32[]{:S(2)}) copy-start(s32[32]{0:T(128)} %param.21) | copy-start | bytes 388
  7.2 192.8 %all-reduce.3.cloned.1.call-start = ((), (), s32[]{:S(2)}) async-start(), calls=%async_computation | async-start | bytes 131072 | tf_op jit(solution)/shard_map/psum | solution.py:61
  78.9 0.6 copy-start.1
  79.6 308.9 %all-reduce.5.cloned.1.call-start = ((), (), s32[]{:S(2)}) async-start(), calls=%async_computation.1 | async-start | bytes 131072 | tf_op jit(solution)/shard_map/psum | solution.py:61
  269.4 0.6 copy-start.2
  270.0 178.4 %all-gather.3.cloned.1.call-start = ((), (), s32[]{:S(2)}) async-start(), calls=%async_computation.2 | async-start | bytes 2162688 | tf_op jit(solution)/shard_map/all_gather | solution.py:80
  270.8 267.9 %all-gather.5.cloned.1.call-start = ((), (), s32[]{:S(2)}) async-start(), calls=%async_computation.3 | async-start | bytes 2162688 | tf_op jit(solution)/shard_map/all_gather | solution.py:80
  428.3 55.1 %copy-start = (f32[16384]{0:T(1024)}, f32[16384]{0:T(1024)S(1)}, u32[]{:S(2)}) copy-start(f32[16384]{0:T(1024)S(1)} %get-tuple-element.1067) | copy-start | bytes 196612
  428.3 55.1 %copy-start.6 = (f32[512]{0:T(512)}, f32[512]{0:T(512)S(1)}, u32[]{:S(2)}) copy-start(f32[512]{0:T(512)S(1)} %get-tuple-element.1081) | copy-start | bytes 6148
Sparse Core Ops, SparseCore 0:
  79.7 120.2 all-reduce.2
  270.1 118.3 all-reduce.4
  391.4 56.9 all-gather.2
  483.5 55.1 all-gather.4
where the time goes:
time: 581 us; the launch traced here: 580 us
  waiting for transfers between devices  313 us (54%)
  other arithmetic  111 us (19%)
  matrix products  70 us (12%)
  loops' own time  52.4 us (9%)
  local copies, waits for them, and re-layouts  19.6 us (3%)
  between operations  13.9 us (2%)
    psum x2, waiting for transfers between devices, on_device(): col_total = lax.psum(col_partial, 'src')  238 us
    all_gather x2, waiting for transfers between devices, on_device(): every_row = lax.all_gather(levels, 'src', axis=0, tiled=True)  75.3 us
    dot_general x2, matrix products, on_device(): jnp.dot(coefficients, columns, preferred_element_type=jnp.float32, precis...  70 us
    reduce_sum x8, other arithmetic, col_part(): return (running + jnp.sum(ratios, axis=0), None)  40.9 us
    reduce_sum x8, other arithmetic, row_part(): return jnp.sum(ratios, axis=1)  39.1 us
    dynamic_update_slice x4, other arithmetic, on_device(): coefficients = lax.map(coeff_block, offsets).reshape(rows_dev, cols_dev)  25 us
    another operation x2, loops' own time, on_device(): lax.scan(col_part, jnp.zeros((cols_dev,), jnp.float32), offsets)  21.1 us
    another operation x2, loops' own time, on_device(): row_partial = lax.map(row_part, offsets).reshape(rows_dev)  20.9 us
  transfers between devices with their start and end apart: 4, of which 4 were waited for; matrix products, arithmetic and copies ran while one was open for 5% of the time, Pallas kernels for 0%

commit v1 on v0

--- a/solution.py
+++ b/solution.py
@@ -3,6 +3,7 @@
 import jax.numpy as jnp
 from jax import lax
 from jax.sharding import PartitionSpec as P
+from jax.lax import axis_size, ppermute
 
 SWEEPS = 2
 ITERS = 2
@@ -10,6 +11,18 @@
 MAP_SIDE = 256
 RANGE = 18
 far_weight = 0.015625
+
+
+def direct_windows(buf):
+    wide_n = axis_size("src")
+    later, v_now = (buf, 0)
+    while 1 << v_now < wide_n:
+        tall = ppermute(
+            later, axis_name="src", perm=tuple(((nth, nth ^ 1 << v_now) for nth in range(wide_n)))
+        )
+        later = later + tall
+        v_now = v_now + 1
+    return later
 
 
 def on_device(out_density, in_density, retention, demand, location, scenario_blocks):
@@ -58,7 +71,7 @@
             return (running + jnp.sum(ratios, axis=0), None)
 
         col_partial, _ = lax.scan(col_part, jnp.zeros((cols_dev,), jnp.float32), offsets)
-        col_total = lax.psum(col_partial, "src")
+        col_total = direct_windows(col_partial)
         in_fit = firms * in_density / col_total
     row_scale = retention / (firms * out_density)
 

time: 581 us -> 373 us (0.64)
  waiting for transfers between devices: 313 us -> 91.2 us
  starting transfers between devices: 0.34 us -> 19.5 us
    psum x2 -> x0, waiting for transfers between devices: 238 us -> none  [on_device(): col_total = lax.psum(col_partial, 'src')]
    ppermute x0 -> x10, waiting for transfers between devices: none -> 22 us  [direct_windows(): ppermute(later, axis_name='src', perm=tuple(((nth, nth ^ 1 << v_now) for...]
    ppermute x0 -> x10, starting transfers between devices: none -> 19.2 us  [direct_windows(): ppermute(later, axis_name='src', perm=tuple(((nth, nth ^ 1 << v_now) for...]
    all_gather x2, waiting for transfers between devices: 75.3 us -> 69.1 us  [on_device(): every_row = lax.all_gather(levels, 'src', axis=0, tiled=True)]
  transfers between devices with their start and end apart: 4 -> 12, of which waited for: 4 -> 12; matrix products, arithmetic and copies ran while one was open for 5% -> 8% of each run, Pallas kernels for 0% -> 0%
where the time goes in v1:
time: 373 us; the launch traced here: 372 us
  other arithmetic  110 us (29%)
  waiting for transfers between devices  91.2 us (24%)
  matrix products  70 us (19%)
  loops' own time  48.8 us (13%)
  starting transfers between devices  19.5 us (5%)
  local copies, waits for them, and re-layouts  18.4 us (5%)
  between operations  14.2 us (4%)
    dot_general x2, matrix products, on_device(): jnp.dot(coefficients, columns, preferred_element_type=jnp.float32, precis...  70 us
    all_gather x2, waiting for transfers between devices, on_device(): every_row = lax.all_gather(levels, 'src', axis=0, tiled=True)  69.1 us
    reduce_sum x8, other arithmetic, col_part(): return (running + jnp.sum(ratios, axis=0), None)  40.8 us
    reduce_sum x8, other arithmetic, row_part(): return jnp.sum(ratios, axis=1)  39.1 us
    dynamic_update_slice x4, other arithmetic, on_device(): coefficients = lax.map(coeff_block, offsets).reshape(rows_dev, cols_dev)  25 us
    ppermute x10, waiting for transfers between devices, direct_windows(): ppermute(later, axis_name='src', perm=tuple(((nth, nth ^ 1 << v_now) for...  22 us
    another operation x2, loops' own time, on_device(): lax.scan(col_part, jnp.zeros((cols_dev,), jnp.float32), offsets)  21.1 us
    ppermute x10, starting transfers between devices, direct_windows(): ppermute(later, axis_name='src', perm=tuple(((nth, nth ^ 1 << v_now) for...  19.2 us
  transfers between devices with their start and end apart: 12, of which 12 were waited for; matrix products, arithmetic and copies ran while one was open for 8% of the time, Pallas kernels for 0%

profile of v1, /device:TPU:0, one launch (start us, length us, event | category | flops | bytes accessed | tf_op | source)
XLA Modules:
  0.0 371.8 jit_solution(18119418969427580277)
XLA Ops:
  10.5 31.7 %while.55 = (s32[]{:T(128)}, f32[4,128]{1,0:T(4,128)S(1)}, s32[4]{0:T(128)S(1)}, s32[]{:T(128)}, s32[512]{0:T(512)S(1)}, /*index=5*/s32[16384]{0:T(1024)S(1)}, s...) while((s32[]{:T(128)}, f32[4,128]{1,0:T(4,128)S(1)}, ...), condition=%wide.region_2.3_spmd.clone, body=%wide.region_0.2_spmd.clone.sunk | while | flops 31457284 | bytes 203979 | solution.py:63
  29.3 4.9 %fusion.33 = f32[128]{0:T(128)S(1)} fusion(f32[128]{0:T(128)S(1)} %dynamic_slice.121, f32[16384]{0:T(1024)S(1)} %get-tuple-element.889, s32[16384]{0:T(1024)S(1)} %get-tuple-element.888, s32[128]{0:T(128)S(1)} %dynamic_slice.122, s32[16384]{0:T(1024)S(1)} %get-tuple-element.886, s32[128]{0:T(128)S(1)} %dynamic_slice.123, s32[128]{0:T(128)S(1)} %iota_add_fusion.11), kind=kLoop, calls=%fused_computation.8.clone.1 | loop fusion | flops 31457152 | bytes 199168 | tf_op jit(solution)/shard_map/while/body/eval_jaxpr/reduce_sum | solution.py:61
  37.2 4.9 %fusion.33 = f32[128]{0:T(128)S(1)} fusion(f32[128]{0:T(128)S(1)} %dynamic_slice.121, f32[16384]{0:T(1024)S(1)} %get-tuple-element.889, s32[16384]{0:T(1024)S(1)} %get-tuple-element.888, s32[128]{0:T(128)S(1)} %dynamic_slice.122, s32[16384]{0:T(1024)S(1)} %get-tuple-element.886, s32[128]{0:T(128)S(1)} %dynamic_slice.123, s32[128]{0:T(128)S(1)} %iota_add_fusion.11), kind=kLoop, calls=%fused_computation.8.clone.1 | loop fusion | flops 31457152 | bytes 199168 | tf_op jit(solution)/shard_map/while/body/eval_jaxpr/reduce_sum | solution.py:61
  42.8 34.3 %while.58 = (s32[]{:T(128)}, f32[16384]{0:T(1024)S(1)}, s32[4]{0:T(128)S(1)}, s32[]{:T(128)}, s32[512]{0:T(512)S(1)}, /*index=5*/s32[16384]{0:T(1024)S(1)}, s32[...) while((s32[]{:T(128)}, f32[16384]{0:T(1024)S(1)}, ...), condition=%wide.region_5.6_spmd.clone, body=%wide.region_3.5_spmd.clone.sunk | while | flops 31473796 | bytes 464593 | solution.py:73
  46.3 5.1 %fusion.36 = f32[16384]{0:T(1024)S(1)} fusion(f32[16384]{0:T(1024)S(1)} %get-tuple-element.929, f32[128]{0:T(128)S(1)} %dynamic_slice.134, s32[16384]{0:T(1024)S(1)} %get-tuple-element.927, s32[128]{0:T(128)S(1)} %dynamic_slice.135, s32[16384]{0:T(1024)S(1)} %get-tuple-element.925, s32[128]{0:T(128)S(1)} %dynamic_slice.136, s32[128]{0:T(128)S(1)} %iota_add_fusion.14), kind=kLoop, calls=%fused_computation.24.clone.1 | loop fusion | flops 31440896 | bytes 264192 | tf_op jit(solution)/shard_map/while/body/eval_jaxpr/reduce_sum | solution.py:71
  54.8 5.1 %fusion.36 = f32[16384]{0:T(1024)S(1)} fusion(f32[16384]{0:T(1024)S(1)} %get-tuple-element.929, f32[128]{0:T(128)S(1)} %dynamic_slice.134, s32[16384]{0:T(1024)S(1)} %get-tuple-element.927, s32[128]{0:T(128)S(1)} %dynamic_slice.135, s32[16384]{0:T(1024)S(1)} %get-tuple-element.925, s32[128]{0:T(128)S(1)} %dynamic_slice.136, s32[128]{0:T(128)S(1)} %iota_add_fusion.14), kind=kLoop, calls=%fused_computation.24.clone.1 | loop fusion | flops 31440896 | bytes 264192 | tf_op jit(solution)/shard_map/while/body/eval_jaxpr/reduce_sum | solution.py:71
  63.4 5.1 %fusion.36 = f32[16384]{0:T(1024)S(1)} fusion(f32[16384]{0:T(1024)S(1)} %get-tuple-element.929, f32[128]{0:T(128)S(1)} %dynamic_slice.134, s32[16384]{0:T(1024)S(1)} %get-tuple-element.927, s32[128]{0:T(128)S(1)} %dynamic_slice.135, s32[16384]{0:T(1024)S(1)} %get-tuple-element.925, s32[128]{0:T(128)S(1)} %dynamic_slice.136, s32[128]{0:T(128)S(1)} %iota_add_fusion.14), kind=kLoop, calls=%fused_computation.24.clone.1 | loop fusion | flops 31440896 | bytes 264192 | tf_op jit(solution)/shard_map/while/body/eval_jaxpr/reduce_sum | solution.py:71
  72.0 5.1 %fusion.36 = f32[16384]{0:T(1024)S(1)} fusion(f32[16384]{0:T(1024)S(1)} %get-tuple-element.929, f32[128]{0:T(128)S(1)} %dynamic_slice.134, s32[16384]{0:T(1024)S(1)} %get-tuple-element.927, s32[128]{0:T(128)S(1)} %dynamic_slice.135, s32[16384]{0:T(1024)S(1)} %get-tuple-element.925, s32[128]{0:T(128)S(1)} %dynamic_slice.136, s32[128]{0:T(128)S(1)} %iota_add_fusion.14), kind=kLoop, calls=%fused_computation.24.clone.1 | loop fusion | flops 31440896 | bytes 264192 | tf_op jit(solution)/shard_map/while/body/eval_jaxpr/reduce_sum | solution.py:71
  99.4 31.7 %while.56 = (s32[]{:T(128)}, f32[4,128]{1,0:T(4,128)S(1)}, s32[4]{0:T(128)S(1)}, s32[]{:T(128)}, s32[512]{0:T(512)S(1)}, /*index=5*/s32[16384]{0:T(1024)S(1)}, s...) while((s32[]{:T(128)}, f32[4,128]{1,0:T(4,128)S(1)}, ...), condition=%wide.region_8.9_spmd.clone, body=%wide.region_6.8_spmd.clone.sunk | while | flops 31457284 | bytes 203979 | solution.py:63
  102.4 4.9 %fusion.34 = f32[128]{0:T(128)S(1)} fusion(f32[128]{0:T(128)S(1)} %dynamic_slice.125, f32[16384]{0:T(1024)S(1)} %get-tuple-element.967, s32[16384]{0:T(1024)S(1)} %get-tuple-element.966, s32[128]{0:T(128)S(1)} %dynamic_slice.126, s32[16384]{0:T(1024)S(1)} %get-tuple-element.964, s32[128]{0:T(128)S(1)} %dynamic_slice.127, s32[128]{0:T(128)S(1)} %iota_add_fusion.12), kind=kLoop, calls=%fused_computation.13.clone.1 | loop fusion | flops 31457152 | bytes 199168 | tf_op jit(solution)/shard_map/while/body/eval_jaxpr/reduce_sum | solution.py:61
  131.8 34.3 %while.59 = (s32[]{:T(128)}, f32[16384]{0:T(1024)S(1)}, s32[4]{0:T(128)S(1)}, s32[]{:T(128)}, s32[512]{0:T(512)S(1)}, /*index=5*/s32[16384]{0:T(1024)S(1)}, s32[...) while((s32[]{:T(128)}, f32[16384]{0:T(1024)S(1)}, ...), condition=%wide.region_11.12_spmd.clone, body=%wide.region_9.11_spmd.clone.sunk | while | flops 31473796 | bytes 464593 | solution.py:73
  135.2 5.1 %fusion.37 = f32[16384]{0:T(1024)S(1)} fusion(f32[16384]{0:T(1024)S(1)} %get-tuple-element.1007, f32[128]{0:T(128)S(1)} %dynamic_slice.138, s32[16384]{0:T(1024)S(1)} %get-tuple-element.1005, s32[128]{0:T(128)S(1)} %dynamic_slice.139, s32[16384]{0:T(1024)S(1)} %get-tuple-element.1003, s32[128]{0:T(128)S(1)} %dynamic_slice.140, s32[128]{0:T(128)S(1)} %iota_add_fusion.15), kind=kLoop, calls=%fused_computation.30.clone.1 | loop fusion | flops 31440896 | bytes 264192 | tf_op jit(solution)/shard_map/while/body/eval_jaxpr/reduce_sum | solution.py:71
  143.8 5.1 %fusion.37 = f32[16384]{0:T(1024)S(1)} fusion(f32[16384]{0:T(1024)S(1)} %get-tuple-element.1007, f32[128]{0:T(128)S(1)} %dynamic_slice.138, s32[16384]{0:T(1024)S(1)} %get-tuple-element.1005, s32[128]{0:T(128)S(1)} %dynamic_slice.139, s32[16384]{0:T(1024)S(1)} %get-tuple-element.1003, s32[128]{0:T(128)S(1)} %dynamic_slice.140, s32[128]{0:T(128)S(1)} %iota_add_fusion.15), kind=kLoop, calls=%fused_computation.30.clone.1 | loop fusion | flops 31440896 | bytes 264192 | tf_op jit(solution)/shard_map/while/body/eval_jaxpr/reduce_sum | solution.py:71
  152.3 5.1 %fusion.37 = f32[16384]{0:T(1024)S(1)} fusion(f32[16384]{0:T(1024)S(1)} %get-tuple-element.1007, f32[128]{0:T(128)S(1)} %dynamic_slice.138, s32[16384]{0:T(1024)S(1)} %get-tuple-element.1005, s32[128]{0:T(128)S(1)} %dynamic_slice.139, s32[16384]{0:T(1024)S(1)} %get-tuple-element.1003, s32[128]{0:T(128)S(1)} %dynamic_slice.140, s32[128]{0:T(128)S(1)} %iota_add_fusion.15), kind=kLoop, calls=%fused_computation.30.clone.1 | loop fusion | flops 31440896 | bytes 264192 | tf_op jit(solution)/shard_map/while/body/eval_jaxpr/reduce_sum | solution.py:71
  160.9 5.1 %fusion.37 = f32[16384]{0:T(1024)S(1)} fusion(f32[16384]{0:T(1024)S(1)} %get-tuple-element.1007, f32[128]{0:T(128)S(1)} %dynamic_slice.138, s32[16384]{0:T(1024)S(1)} %get-tuple-element.1005, s32[128]{0:T(128)S(1)} %dynamic_slice.139, s32[16384]{0:T(1024)S(1)} %get-tuple-element.1003, s32[128]{0:T(128)S(1)} %dynamic_slice.140, s32[128]{0:T(128)S(1)} %iota_add_fusion.15), kind=kLoop, calls=%fused_computation.30.clone.1 | loop fusion | flops 31440896 | bytes 264192 | tf_op jit(solution)/shard_map/while/body/eval_jaxpr/reduce_sum | solution.py:71
  187.0 38.8 %while.57 = (s32[]{:T(128)}, f32[4,128,16384]{2,1,0:T(8,128)}, s32[4]{0:T(128)S(1)}, f32[512]{0:T(512)S(1)}, f32[16384]{0:T(1024)S(1)}, /*index=5*/s32[]{:T(128)...) while((s32[]{:T(128)}, f32[4,128,16384]{2,1,0:T(8,128)}, ...), condition=%wide.region_13.14_spmd.clone, body=%wide.region_12.13_spmd.clone.sunk | while | flops 29360260 | bytes 8593107 | solution.py:85
  190.5 6.3 %fusion.35 = f32[4,128,16384]{2,1,0:T(8,128)} fusion(f32[4,128,16384]{2,1,0:T(8,128)} %get-tuple-element.1026, s32[]{:T(128)} %get-tuple-element.1025, f32[128]{0:T(128)S(1)} %dynamic_slice.129, s32[16384]{0:T(1024)S(1)} %get-tuple-element.1048, s32[128]{0:T(128)S(1)} %dynamic_slice.130, s32[16384]{0:T(1024)S(1)} %get-tuple-element.1046, ...), kind=kLoop, calls=%fused_computation.17.clone.1 | loop fusion | flops 29360128 | bytes 8588288 | tf_op jit(solution)/shard_map/while/body/jit(dynamic_update_index_in_dim)/dynamic_update_slice | solution.py:85
  200.2 6.2 %fusion.35 = f32[4,128,16384]{2,1,0:T(8,128)} fusion(f32[4,128,16384]{2,1,0:T(8,128)} %get-tuple-element.1026, s32[]{:T(128)} %get-tuple-element.1025, f32[128]{0:T(128)S(1)} %dynamic_slice.129, s32[16384]{0:T(1024)S(1)} %get-tuple-element.1048, s32[128]{0:T(128)S(1)} %dynamic_slice.130, s32[16384]{0:T(1024)S(1)} %get-tuple-element.1046, ...), kind=kLoop, calls=%fused_computation.17.clone.1 | loop fusion | flops 29360128 | bytes 8588288 | tf_op jit(solution)/shard_map/while/body/jit(dynamic_update_index_in_dim)/dynamic_update_slice | solution.py:85
  209.9 6.3 %fusion.35 = f32[4,128,16384]{2,1,0:T(8,128)} fusion(f32[4,128,16384]{2,1,0:T(8,128)} %get-tuple-element.1026, s32[]{:T(128)} %get-tuple-element.1025, f32[128]{0:T(128)S(1)} %dynamic_slice.129, s32[16384]{0:T(1024)S(1)} %get-tuple-element.1048, s32[128]{0:T(128)S(1)} %dynamic_slice.130, s32[16384]{0:T(1024)S(1)} %get-tuple-element.1046, ...), kind=kLoop, calls=%fused_computation.17.clone.1 | loop fusion | flops 29360128 | bytes 8588288 | tf_op jit(solution)/shard_map/while/body/jit(dynamic_update_index_in_dim)/dynamic_update_slice | solution.py:85
  219.6 6.2 %fusion.35 = f32[4,128,16384]{2,1,0:T(8,128)} fusion(f32[4,128,16384]{2,1,0:T(8,128)} %get-tuple-element.1026, s32[]{:T(128)} %get-tuple-element.1025, f32[128]{0:T(128)S(1)} %dynamic_slice.129, s32[16384]{0:T(1024)S(1)} %get-tuple-element.1048, s32[128]{0:T(128)S(1)} %dynamic_slice.130, s32[16384]{0:T(1024)S(1)} %get-tuple-element.1046, ...), kind=kLoop, calls=%fused_computation.17.clone.1 | loop fusion | flops 29360128 | bytes 8588288 | tf_op jit(solution)/shard_map/while/body/jit(dynamic_update_index_in_dim)/dynamic_update_slice | solution.py:85
  225.8 13.8 %all-gather.3.cloned.1.call-done = f32[16384,32]{0,1:T(8,128)} async-done(((f32[512,32]{0,1:T(8,128)}), f32[16384,32]{0,1:T(8,128)}) %all-gather.3.cloned.1.call-update) | async-done | bytes 2097168 | tf_op jit(solution)/shard_map/all_gather | solution.py:93
  239.6 35.0 %fusion.17 = f32[512,32]{0,1:T(8,128)} fusion(f32[512,16384]{1,0:T(8,128)} %bitcast.30, f32[16384,32]{0,1:T(8,128)} %all-gather.3.cloned.1.call-done, f32[512]{0:T(512)S(1)} %copy-done.2, s32[512]{0:T(512)S(1)} %add_select_fusion.2, s32[32]{0:T(128)S(1)} %copy-done.3), kind=kOutput, calls=%fused_computation.36 | convolution fusion | flops 3221274624 | bytes 35721344 | tf_op jit(solution)/shard_map/dot_general | solution.py:96
  274.7 55.3 %all-gather.5.cloned.1.call-done = f32[16384,32]{0,1:T(8,128)} async-done(((f32[512,32]{0,1:T(8,128)}), f32[16384,32]{0,1:T(8,128)}) %all-gather.5.cloned.1.call-update) | async-done | bytes 2097168 | tf_op jit(solution)/shard_map/all_gather | solution.py:93
  330.0 35.0 %fusion.16 = f32[512,32]{0,1:T(8,128)} fusion(f32[512,16384]{1,0:T(8,128)} %bitcast.31, f32[16384,32]{0,1:T(8,128)} %all-gather.5.cloned.1.call-done, f32[512]{0:T(512)S(1)} %copy-done.2, s32[512]{0:T(512)S(1)} %add_select_fusion.2, s32[32]{0:T(128)S(1)} %copy-done.3), kind=kOutput, calls=%fused_computation.34 | convolution fusion | flops 3221274624 | bytes 35721344 | tf_op jit(solution)/shard_map/dot_general | solution.py:96
  (183 shorter events, 89.3 us)
Async XLA Ops:
  7.2 179.8 %copy-start.1 = (f32[16384]{0:T(1024)S(1)}, f32[16384]{0:T(1024)}, u32[]{:S(2)}) copy-start(f32[16384]{0:T(1024)} %param.17) | copy-start | bytes 196612
  7.2 176.9 %copy-start.2 = (f32[512]{0:T(512)S(1)}, f32[512]{0:T(512)}, u32[]{:S(2)}) copy-start(f32[512]{0:T(512)} %param.19) | copy-start | bytes 6148
  7.2 176.8 %copy-start.3 = (s32[32]{0:T(128)S(1)}, s32[32]{0:T(128)}, u32[]{:S(2)}) copy-start(s32[32]{0:T(128)} %param.21) | copy-start | bytes 388
  7.2 232.4 %all-gather.3.cloned.1.call-start = ((), (), s32[]{:S(2)}) async-start(), calls=%async_computation | async-start | bytes 2162688 | tf_op jit(solution)/shard_map/all_gather | solution.py:93
  77.1 1.4 collective-permute-start
  78.5 5.3 %collective-permute-start.1 = (f32[16384]{0:T(1024)S(1)}, f32[16384]{0:T(1024)S(1)}, u32[]{:S(2)}, u32[]{:S(2)}) collective-permute-start(f32[16384]{0:T(1024)S(1)} %add.246), channel_id=1, source_target_pairs={{0,2},{1,3},{2,0},{3,1},{4,6},{5,7},{6,4},{7,5},{8,10},{9,11},{10,... | collective-permute-start | bytes 196616 | tf_op jit(solution)/shard_map/ppermute | solution.py:20
  83.9 4.3 %collective-permute-start.2 = (f32[16384]{0:T(1024)S(1)}, f32[16384]{0:T(1024)S(1)}, u32[]{:S(2)}, u32[]{:S(2)}) collective-permute-start(f32[16384]{0:T(1024)S(1)} %add.247), channel_id=1, source_target_pairs={{0,4},{1,5},{2,6},{3,7},{4,0},{5,1},{6,2},{7,3},{8,12},{9,13},{10,... | collective-permute-start | bytes 196616 | tf_op jit(solution)/shard_map/ppermute | solution.py:20
  88.2 4.3 %collective-permute-start.3 = (f32[16384]{0:T(1024)S(1)}, f32[16384]{0:T(1024)S(1)}, u32[]{:S(2)}, u32[]{:S(2)}) collective-permute-start(f32[16384]{0:T(1024)S(1)} %add.248), channel_id=1, source_target_pairs={{0,8},{1,9},{2,10},{3,11},{4,12},{5,13},{6,14},{7,15},{8,0},{9,1},... | collective-permute-start | bytes 196616 | tf_op jit(solution)/shard_map/ppermute | solution.py:20
  92.6 5.9 %collective-permute-start.4 = (f32[16384]{0:T(1024)S(1)}, f32[16384]{0:T(1024)S(1)}, u32[]{:S(2)}, u32[]{:S(2)}) collective-permute-start(f32[16384]{0:T(1024)S(1)} %add.249), channel_id=1, source_target_pairs={{0,16},{1,17},{2,18},{3,19},{4,20},{5,21},{6,22},{7,23},{8,24},{9,... | collective-permute-start | bytes 196616 | tf_op jit(solution)/shard_map/ppermute | solution.py:20
  166.0 1.3 collective-permute-start.5
  167.4 4.3 %collective-permute-start.6 = (f32[16384]{0:T(1024)S(1)}, f32[16384]{0:T(1024)S(1)}, u32[]{:S(2)}, u32[]{:S(2)}) collective-permute-start(f32[16384]{0:T(1024)S(1)} %add.251), channel_id=1, source_target_pairs={{0,2},{1,3},{2,0},{3,1},{4,6},{5,7},{6,4},{7,5},{8,10},{9,11},{10,... | collective-permute-start | bytes 196616 | tf_op jit(solution)/shard_map/ppermute | solution.py:20
  171.7 4.3 %collective-permute-start.7 = (f32[16384]{0:T(1024)S(1)}, f32[16384]{0:T(1024)S(1)}, u32[]{:S(2)}, u32[]{:S(2)}) collective-permute-start(f32[16384]{0:T(1024)S(1)} %add.252), channel_id=1, source_target_pairs={{0,4},{1,5},{2,6},{3,7},{4,0},{5,1},{6,2},{7,3},{8,12},{9,13},{10,... | collective-permute-start | bytes 196616 | tf_op jit(solution)/shard_map/ppermute | solution.py:20
  176.1 4.3 %collective-permute-start.8 = (f32[16384]{0:T(1024)S(1)}, f32[16384]{0:T(1024)S(1)}, u32[]{:S(2)}, u32[]{:S(2)}) collective-permute-start(f32[16384]{0:T(1024)S(1)} %add.253), channel_id=1, source_target_pairs={{0,8},{1,9},{2,10},{3,11},{4,12},{5,13},{6,14},{7,15},{8,0},{9,1},... | collective-permute-start | bytes 196616 | tf_op jit(solution)/shard_map/ppermute | solution.py:20
  180.4 6.6 %collective-permute-start.9 = (f32[16384]{0:T(1024)S(1)}, f32[16384]{0:T(1024)S(1)}, u32[]{:S(2)}, u32[]{:S(2)}) collective-permute-start(f32[16384]{0:T(1024)S(1)} %add.254), channel_id=1, source_target_pairs={{0,16},{1,17},{2,18},{3,19},{4,20},{5,21},{6,22},{7,23},{8,24},{9,... | collective-permute-start | bytes 196616 | tf_op jit(solution)/shard_map/ppermute | solution.py:20
  184.8 145.2 %all-gather.5.cloned.1.call-start = ((), (), s32[]{:S(2)}) async-start(), calls=%async_computation.1 | async-start | bytes 2162688 | tf_op jit(solution)/shard_map/all_gather | solution.py:93
  225.8 48.8 %copy-start = (f32[16384]{0:T(1024)}, f32[16384]{0:T(1024)S(1)}, u32[]{:S(2)}) copy-start(f32[16384]{0:T(1024)S(1)} %get-tuple-element.1065) | copy-start | bytes 196612
  225.8 48.8 %copy-start.4 = (f32[512]{0:T(512)}, f32[512]{0:T(512)S(1)}, u32[]{:S(2)}) copy-start(f32[512]{0:T(512)S(1)} %get-tuple-element.1093) | copy-start | bytes 6148
Sparse Core Ops, SparseCore 0:
  184.9 54.7 all-gather.2
  274.8 55.1 all-gather.4
